TPU v7x, 32 devices: a whole 2x2x4 slice. The times are simulated.
32 devices in a mesh: ctx: 8 (over z, core), tp: 4 (over y, x).
Axes of the slice: x: 2, y: 2, z: 4, core: 2. Of those that a mesh axis runs over, the one named last changes fastest.
Arguments:
- query_latent: bfloat16 [4096, 64, 512], P('ctx', 'tp'), may hold values from -24 to 24
- query_rope: bfloat16 [4096, 4096], P('ctx', 'tp'), may hold values from -24 to 24
- key_latent: bfloat16 [4096, 512], P('ctx'), may hold values from -6 to 6
- key_rope: bfloat16 [2048, 128], P('ctx'), may hold values from -6 to 6
- block_ids: int32 [16], replicated, may hold values from 0 to 15, as said below
- value_up: bfloat16 [64, 512, 128], P('tp'), may hold values from -0.5 to 0.5
- out_weight: bfloat16 [8192, 7168], P('tp'), may hold values from -0.0625 to 0.0625
- residual: bfloat16 [4096, 7168], P(('ctx', 'tp')), may hold values from -18 to 18
- norm_gain: float32 [7168], replicated, may hold values from 0.1 to 1.9
- gate_weight: bfloat16 [7168, 2048], P('ctx', 'tp'), may hold values from -0.0625 to 0.0625
- up_weight: bfloat16 [7168, 2048], P('ctx', 'tp'), may hold values from -0.0625 to 0.0625
- down_weight: bfloat16 [7168, 2048], P('ctx', 'tp'), may hold values from -0.125 to 0.125
Outputs:
- layer_out: bfloat16 [4096, 7168], P(('ctx', 'tp'))
Inputs may be any that keep to these rules, and one draw needn't show every extreme that they name: `block_ids`: index c of ctx stores blocks 2c and 2c + 1; their two entries sum to 15, and every value appears once.
All inputs are finite; a program needn't handle non-finite values.
Results may differ from a plain program's by a relative error of at most 0.018.
Values may be sent and summed in bfloat16 or wider, within the bound.
A program may use at most 192 MiB of HBM per device.

v0:
```python
import jax
import jax.numpy as jnp
from jax import lax
from jax.sharding import PartitionSpec as P


def from_behind(x, axis, by):
    length = lax.axis_size(axis)
    return lax.ppermute(x, axis, [(i, (i + by) % length) for i in range(length)])


def rms_norm(activation, gain_vector):
    mean_square = jnp.mean(activation * activation, axis=-1, keepdims=True)
    return (activation * lax.rsqrt(mean_square + 1e-06) * gain_vector).astype(jnp.bfloat16)


def local(
    query_latent,
    query_rope,
    key_latent,
    key_rope,
    block_ids,
    value_up,
    out_weight,
    residual,
    norm_gain,
    gate_weight,
    up_weight,
    down_weight,
):
    seq_rows = key_latent.shape[0]
    half_len = seq_rows // 2
    head_count = query_latent.shape[1]
    rope_dim = key_rope.shape[1] // 2
    head_dim = value_up.shape[2]
    ctx_count = lax.axis_size("ctx")
    tp_count = lax.axis_size("tp")
    score_scale = (head_dim + rope_dim) ** (-0.5)
    recv_latent, recv_rope = from_behind((key_latent, key_rope), "ctx", 1)
    keys_lat = jnp.concatenate([key_latent, recv_latent], axis=0)
    keys_rot = jnp.concatenate(
        [key_rope.reshape(seq_rows, rope_dim), recv_rope.reshape(seq_rows, rope_dim)], axis=0
    )
    current = lax.axis_index("ctx")
    previous = (current + ctx_count - 1) % ctx_count
    own_ids = lax.dynamic_slice_in_dim(block_ids, current * 2, 2, 0)
    prev_ids = lax.dynamic_slice_in_dim(block_ids, previous * 2, 2, 0)
    row_index = jnp.arange(seq_rows, dtype=jnp.int32)
    first_half = row_index < half_len
    offset = row_index % half_len
    query_pos = jnp.where(first_half, own_ids[0], own_ids[1]) * half_len + offset
    key_pos = jnp.concatenate(
        [query_pos, jnp.where(first_half, prev_ids[0], prev_ids[1]) * half_len + offset], axis=0
    )
    rope_queries = query_rope.reshape(seq_rows, head_count, rope_dim)
    block_rows = min(seq_rows, 512)

    def attend(block_index):
        scores = jnp.einsum(
            "shl,kl->hsk", query_latent, keys_lat, preferred_element_type=jnp.float32
        )
        scores = scores + jnp.einsum(
            "shr,kr->hsk", rope_queries, keys_rot, preferred_element_type=jnp.float32
        )
        scores = scores * score_scale
        visible = key_pos[None, :] <= query_pos[:, None]
        scores = jnp.where(visible[None], scores, -jnp.inf)
        highest = jnp.max(scores, axis=-1, keepdims=True)
        exponent = jnp.exp(scores - highest)
        weights = (exponent / jnp.sum(exponent, axis=-1, keepdims=True)).astype(jnp.bfloat16)
        blended = jnp.einsum(
            "hsk,kl->shl", weights, keys_lat, preferred_element_type=jnp.float32
        ).astype(jnp.bfloat16)
        values = jnp.einsum(
            "shl,hlv->shv", blended, value_up, preferred_element_type=jnp.float32
        ).astype(jnp.bfloat16)
        return values.reshape(block_rows, head_count * head_dim)

    head_out = lax.map(attend, jnp.arange(seq_rows // block_rows, dtype=jnp.int32)).reshape(
        seq_rows, head_count * head_dim
    )
    share_rows = seq_rows // tp_count
    tp_index = lax.axis_index("tp")
    partial_attn = jnp.dot(head_out, out_weight, preferred_element_type=jnp.float32)
    attn_total = lax.psum(partial_attn.astype(jnp.bfloat16), "tp").astype(jnp.float32)
    all_residual = lax.all_gather(residual, "tp", axis=0, tiled=True)
    hidden_state = all_residual.astype(jnp.float32) + attn_total
    normed_all = rms_norm(hidden_state, norm_gain)
    own_state = lax.dynamic_slice_in_dim(hidden_state, tp_index * share_rows, share_rows, 0)
    gate_full, up_full, down_full = (
        lax.all_gather(gate_weight, "ctx", axis=0, tiled=True),
        lax.all_gather(up_weight, "ctx", axis=0, tiled=True),
        lax.all_gather(down_weight, "ctx", axis=0, tiled=True),
    )
    gate_proj = jnp.dot(normed_all, gate_full, preferred_element_type=jnp.float32)
    up_proj = jnp.dot(normed_all, up_full, preferred_element_type=jnp.float32)
    hidden_units = (jax.nn.silu(gate_proj) * up_proj).astype(jnp.bfloat16)
    shared_part = lax.psum_scatter(
        lax.dot_general(
            hidden_units, down_full, (((1,), (1,)), ((), ())), preferred_element_type=jnp.float32
        ).astype(jnp.bfloat16),
        "tp",
        scatter_dimension=0,
        tiled=True,
    ).astype(jnp.float32)
    return (own_state + shared_part).astype(jnp.bfloat16)


def solution(mesh):
    placed = (
        P("ctx", "tp", None),
        P("ctx", "tp"),
        P("ctx", None),
        P("ctx", None),
        P(),
        P("tp", None, None),
        P("tp", None),
        P(("ctx", "tp"), None),
        P(),
        P("ctx", "tp"),
        P("ctx", "tp"),
        P("ctx", "tp"),
    )
    return jax.shard_map(
        local, mesh=mesh, in_specs=placed, out_specs=P(("ctx", "tp"), None), check_vma=False
    )
```

profile of v0, /device:TPU:0, one launch (start us, length us, event | category | flops | bytes accessed | tf_op | source)
XLA Modules:
  0.0 672.1 jit_solution(7638917272089841626)
XLA Ops:
  6.5 0.0 copy-start
  6.5 0.0 all-reduce.2.cloned.1.call-start
  6.5 0.5 collective-permute-start
  7.0 2.7 collective-permute-start.1
  9.7 0.8 fusion.35
  10.5 0.6 fusion.34
  11.1 1.2 fusion.22
  12.3 1.3 multiply_add_fusion
  13.6 1.2 broadcast_compare_fusion
  14.8 0.9 reshape.69
  15.7 1.5 copy.19
  17.2 0.1 copy.17
  17.3 1.5 collective-permute-done.1
  18.8 0.1 reshape.70
  18.9 0.1 copy.18
  19.0 0.0 collective-permute-done
  19.0 18.1 %fusion.3 = f32[1024,512,16]{1,0,2:T(8,128)} fusion(bf16[512,16,512]{2,1,0:T(8,128)(2,1)} %param.12, bf16[512,512]{1,0:T(8,128)(2,1)} %collective-permute-done, bf16[512,512]{1,0:T(8,128)(2,1)} %param.14), kind=kOutput, calls=%fused_computation.11 | convolution fusion | flops 8592031744 | bytes 42991616 | tf_op jit(solution)/shard_map/while/body/eval_jaxpr/shl,kl->hsk/dot_general | solution.py:59
  37.1 24.3 %fusion.37 = (f32[16,512]{1,0:T(8,128)S(1)}, f32[16,512,1024]{1,2,0:T(8,128)}) fusion(f32[1024,512,16]{1,0,2:T(8,128)} %fusion.3, pred[512,1024]{0,1:T(8,128)(4,1)} %broadcast_compare_fusion, bf16[512,16,64]{0,2,1:T(8,128)(2,1)S(1)} %bitcast.36, bf16[512,64]{0,1:T(8,128)(2,1)S(1)} %copy.18, bf16[512,64]{0,1:T(8,128)(2,1)S(1)} %copy.17), kind=kOutput, calls=%fused_computation.51 | convolution fusion | flops 1115948032 | bytes 68845568 | tf_op jit(solution)/shard_map/while/body/eval_jaxpr/sub | solution.py:69
  61.3 0.0 copy-done
  61.3 17.5 %fusion.9 = bf16[16,512,128]{1,2,0:T(8,128)(2,1)} fusion(bf16[16,512,128]{2,1,0:T(8,128)(2,1)S(1)} %copy-done, f32[16,512,1024]{1,2,0:T(8,128)} %get-tuple-element.41, f32[16,512]{1,0:T(8,128)S(1)} %get-tuple-element.40, bf16[512,512]{1,0:T(8,128)(2,1)} %collective-permute-done, bf16[512,512]{1,0:T(8,128)(2,1)} %param.14), kind=kOutput, calls=%fused_computation.17 | convolution fusion | flops 9687793664 | bytes 38830080 | tf_op jit(solution)/shard_map/while/body/eval_jaxpr/shl,hlv->shv/dot_general | solution.py:74
  78.9 23.3 %convolution_convert_fusion.1 = bf16[512,7168]{1,0:T(8,128)(2,1)} fusion(bf16[512,2048]{0,1:T(8,128)(2,1)} %bitcast.37, bf16[2048,7168]{1,0:T(8,128)(2,1)} %param.18), kind=kOutput, calls=%fused_computation.10 | convolution fusion | flops 15036055552 | bytes 38797312 | tf_op jit(solution)/shard_map/dot_general | solution.py:84
  102.2 0.0 all-reduce.2.cloned.1.call-update
  102.2 0.0 all-gather.5.cloned.1.call-start
  102.3 0.7 all-gather.5.cloned.1.call-update
  103.0 0.0 all-gather.7.cloned.1.call-start
  103.0 0.7 all-gather.7.cloned.1.call-update
  103.7 0.0 all-gather.11.cloned.1.call-start
  103.7 0.5 all-gather.11.cloned.1.call-update
  104.3 0.0 all-gather.9.cloned.1.call-start
  104.3 0.5 all-gather.9.cloned.1.call-update
  104.9 0.0 copy-start.2
  104.9 0.0 reduce-scatter.2.cloned.1.call-start
  104.9 153.2 %all-reduce.2.cloned.1.call-done = bf16[512,7168]{1,0:T(8,128)(2,1)} async-done(((bf16[512,7168]{1,0:T(8,128)(2,1)}), bf16[512,7168]{1,0:T(8,128)(2,1)}) %all-reduce.2.cloned.1.call-update) | async-done | bytes 7340048 | tf_op jit(solution)/shard_map/psum | solution.py:85
  258.1 80.8 %all-gather.5.cloned.1.call-done = bf16[512,7168]{1,0:T(8,128)(2,1)} async-done(((bf16[128,7168]{1,0:T(8,128)(2,1)}), bf16[512,7168]{1,0:T(8,128)(2,1)}) %all-gather.5.cloned.1.call-update) | async-done | bytes 7340048 | tf_op jit(solution)/shard_map/all_gather | solution.py:86
  338.9 13.5 %convert_add_fusion = (f32[512,7168]{1,0:T(8,128)}, f32[512]{0:T(512)S(1)}) fusion(bf16[512,7168]{1,0:T(8,128)(2,1)} %all-reduce.2.cloned.1.call-done, bf16[512,7168]{1,0:T(8,128)(2,1)} %all-gather.5.cloned.1.call-done), kind=kLoop, calls=%fused_computation.7 | loop fusion | flops 18349568 | bytes 29362176 | tf_op jit(solution)/shard_map/add | solution.py:87
  352.4 61.6 %all-gather.7.cloned.1.call-done = bf16[7168,512]{1,0:T(8,128)(2,1)} async-done(((bf16[896,512]{1,0:T(8,128)(2,1)}), bf16[7168,512]{1,0:T(8,128)(2,1)}) %all-gather.7.cloned.1.call-update) | async-done | bytes 7340048 | tf_op jit(solution)/shard_map/all_gather | solution.py:91
  413.9 0.0 copy-done.2
  413.9 9.7 %fusion.33 = f32[512,512]{1,0:T(8,128)S(1)} fusion(bf16[7168,512]{1,0:T(8,128)(2,1)} %all-gather.7.cloned.1.call-done, f32[7168]{0:T(1024)S(1)} %copy-done.2, f32[512]{0:T(512)S(1)} %add_rsqrt_fusion, bf16[512,7168]{1,0:T(8,128)(2,1)} %all-reduce.2.cloned.1.call-done, bf16[512,7168]{1,0:T(8,128)(2,1)} %all-gather.5.cloned.1.call-done), kind=kOutput, calls=%fused_computation.47 | convolution fusion | flops 3780116480 | bytes 23099392 | tf_op jit(solution)/shard_map/dot_general | solution.py:95
  423.7 63.8 %all-gather.11.cloned.1.call-done = bf16[7168,512]{1,0:T(8,128)(2,1)} async-done(((bf16[896,512]{1,0:T(8,128)(2,1)}), bf16[7168,512]{1,0:T(8,128)(2,1)}) %all-gather.11.cloned.1.call-update) | async-done | bytes 7340048 | tf_op jit(solution)/shard_map/all_gather | solution.py:93
  487.5 73.5 %all-gather.9.cloned.1.call-done = bf16[7168,512]{1,0:T(8,128)(2,1)} async-done(((bf16[896,512]{1,0:T(8,128)(2,1)}), bf16[7168,512]{1,0:T(8,128)(2,1)}) %all-gather.9.cloned.1.call-update) | async-done | bytes 7340048 | tf_op jit(solution)/shard_map/all_gather | solution.py:92
  561.0 22.3 %convolution_convert_fusion = bf16[512,7168]{1,0:T(8,128)(2,1)} fusion(bf16[7168,512]{1,0:T(8,128)(2,1)} %all-gather.11.cloned.1.call-done, bf16[7168,512]{1,0:T(8,128)(2,1)} %all-gather.9.cloned.1.call-done, f32[512,512]{1,0:T(8,128)S(1)} %fusion.33, f32[7168]{0:T(1024)S(1)} %copy-done.2, f32[512]{0:T(512)S(1)} %add_rsqrt_fusion, ...), kind=kOutput, calls=%fused_computation.9 | convolution fusion | flops 7543455744 | bytes 37779456 | tf_op jit(solution)/shard_map/dot_general | solution.py:99
  583.3 0.0 copy-start.1
  583.3 0.0 reduce-scatter.2.cloned.1.call-update
  583.3 77.7 %reduce-scatter.2.cloned.1.call-done = bf16[128,7168]{1,0:T(8,128)(2,1)} async-done(((bf16[512,7168]{1,0:T(8,128)(2,1)}), bf16[128,7168]{1,0:T(8,128)(2,1)}) %reduce-scatter.2.cloned.1.call-update) | async-done | bytes 1835024 | tf_op jit(solution)/shard_map/reduce_scatter | solution.py:98
  661.1 4.2 add_convert_fusion
  665.2 0.0 copy-done.1
  (2 shorter events, 0.0 us)
Async XLA Ops:
  6.5 54.8 %copy-start = (bf16[16,512,128]{2,1,0:T(8,128)(2,1)S(1)}, bf16[16,512,128]{2,1,0:T(8,128)(2,1)}, u32[]{:S(2)}) copy-start(bf16[16,512,128]{2,1,0:T(8,128)(2,1)} %param.17) | copy-start | bytes 6291460
  6.5 251.6 %all-reduce.2.cloned.1.call-start = ((), (), s32[]{:S(2)}) async-start(), calls=%async_computation.2 | async-start | bytes 14680064 | tf_op jit(solution)/shard_map/psum | solution.py:85
  6.5 12.5 %collective-permute-start = (bf16[512,512]{1,0:T(8,128)(2,1)}, bf16[512,512]{1,0:T(8,128)(2,1)}, u32[]{:S(2)}, u32[]{:S(2)}) collective-permute-start(bf16[512,512]{1,0:T(8,128)(2,1)} %param.14), channel_id=1, source_target_pairs={{0,4},{4,8},{8,12},{12,16},{16,20},{20,24},{24,28},{28,0},{1,5},{5... | collective-permute-start | bytes 1572872 | tf_op jit(solution)/shard_map/ppermute | solution.py:9
  7.0 11.8 %collective-permute-start.1 = (bf16[256,128]{1,0:T(8,128)(2,1)}, bf16[256,128]{1,0:T(8,128)(2,1)S(1)}, u32[]{:S(2)}, u32[]{:S(2)}) collective-permute-start(bf16[256,128]{1,0:T(8,128)(2,1)} %param.15), channel_id=1, source_target_pairs={{0,4},{4,8},{8,12},{12,16},{16,20},{20,24},{24,28},{28,0},{1,5},{5... | collective-permute-start | bytes 196616 | tf_op jit(solution)/shard_map/ppermute | solution.py:9
  102.2 236.6 %all-gather.5.cloned.1.call-start = ((), (), s32[]{:S(2)}) async-start(), calls=%async_computation.1 | async-start | bytes 9175040 | tf_op jit(solution)/shard_map/all_gather | solution.py:86
  103.0 311.0 %all-gather.7.cloned.1.call-start = ((), (), s32[]{:S(2)}) async-start(), calls=%async_computation.3 | async-start | bytes 8257536 | tf_op jit(solution)/shard_map/all_gather | solution.py:91
  103.7 383.8 %all-gather.11.cloned.1.call-start = ((), (), s32[]{:S(2)}) async-start(), calls=%async_computation.5 | async-start | bytes 8257536 | tf_op jit(solution)/shard_map/all_gather | solution.py:93
  104.3 456.7 %all-gather.9.cloned.1.call-start = ((), (), s32[]{:S(2)}) async-start(), calls=%async_computation.4 | async-start | bytes 8257536 | tf_op jit(solution)/shard_map/all_gather | solution.py:92
  104.9 309.1 %copy-start.2 = (f32[7168]{0:T(1024)S(1)}, f32[7168]{0:T(1024)}, u32[]{:S(2)}) copy-start(f32[7168]{0:T(1024)} %param.20) | copy-start | bytes 86020
  104.9 556.2 %reduce-scatter.2.cloned.1.call-start = ((), (), s32[]{:S(2)}) async-start(), calls=%async_computation.6 | async-start | bytes 9175040 | tf_op jit(solution)/shard_map/reduce_scatter | solution.py:98
  583.3 81.9 %copy-start.1 = (bf16[16,512,128]{2,1,0:T(8,128)(2,1)S(1)}, bf16[16,512,128]{2,1,0:T(8,128)(2,1)}, u32[]{:S(2)}) copy-start(bf16[16,512,128]{2,1,0:T(8,128)(2,1)} %param.17) | copy-start | bytes 6291460
Sparse Core Ops, SparseCore 0:
  102.3 155.7 all-reduce.1
  259.9 78.8 all-gather.4
  340.5 73.3 all-gather.6
  415.4 71.9 all-gather.10
  489.0 71.9 all-gather.8
  583.5 77.5 reduce-scatter.1
where the time goes:
time: 672 us
  waiting for transfers between devices  515 us (77%)
  matrix products  115 us (17%)
  other arithmetic  21.3 us (3%)
  between operations  13.6 us (2%)
    psum x1, waiting for transfers between devices, local(): lax.psum(partial_attn.astype(jnp.bfloat16), 'tp').astype(jnp.float32)  153 us
    all_gather x1, waiting for transfers between devices, local(): all_residual = lax.all_gather(residual, 'tp', axis=0, tiled=True)  80.8 us
    reduce_scatter x1, waiting for transfers between devices, local(): lax.psum_scatter(lax.dot_general(hidden_units, down_full, (((1,), (1,)),...  77.7 us
    all_gather x1, waiting for transfers between devices, local(): lax.all_gather(up_weight, 'ctx', axis=0, tiled=True)  73.5 us
    all_gather x1, waiting for transfers between devices, local(): lax.all_gather(down_weight, 'ctx', axis=0, tiled=True)  63.8 us
    all_gather x1, waiting for transfers between devices, local(): lax.all_gather(gate_weight, 'ctx', axis=0, tiled=True)  61.6 us
    sub x1, matrix products, attend(): exponent = jnp.exp(scores - highest)  24.3 us
    dot_general x1, matrix products, local(): jnp.dot(head_out, out_weight, preferred_element_type=jnp.float32)  23.3 us
  transfers between devices with their start and end apart: 8, of which 7 were waited for; matrix products, arithmetic and copies ran while one was open for 5% of the time, Pallas kernels for 0%

commit v1 on v0

--- a/solution.py
+++ b/solution.py
@@ -83,7 +83,12 @@
     tp_index = lax.axis_index("tp")
     partial_attn = jnp.dot(head_out, out_weight, preferred_element_type=jnp.float32)
     attn_total = lax.psum(partial_attn.astype(jnp.bfloat16), "tp").astype(jnp.float32)
-    all_residual = lax.all_gather(residual, "tp", axis=0, tiled=True)
+    ring = [residual]
+    for hop in range(3):
+        ring.append(lax.ppermute(ring[-1], "tp", [(dev, (dev + 1) % 4) for dev in range(4)]))
+    all_residual = jnp.roll(
+        jnp.concatenate(ring[::-1], axis=0), (lax.axis_index("tp") + 1) * ring[0].shape[0], axis=0
+    )
     hidden_state = all_residual.astype(jnp.float32) + attn_total
     normed_all = rms_norm(hidden_state, norm_gain)
     own_state = lax.dynamic_slice_in_dim(hidden_state, tp_index * share_rows, share_rows, 0)

time: 672 us -> 480 us (0.71)
  waiting for transfers between devices: 515 us -> 294 us
  local copies, waits for them, and re-layouts: 4.16 us -> 24.6 us
    ppermute x0 -> x3, waiting for transfers between devices: none -> 203 us  [local(): lax.ppermute(ring[-1], 'tp', [(dev, (dev + 1) % 4) for dev in range(4)])]
    psum x1, waiting for transfers between devices: 153 us -> 8.62 us  [local(): lax.psum(partial_attn.astype(jnp.bfloat16), 'tp').astype(jnp.float32)]
    all_gather x1 -> x0, waiting for transfers between devices: 80.8 us -> none  [local(): all_residual = lax.all_gather(residual, 'tp', axis=0, tiled=True)]
    all_gather x1, waiting for transfers between devices: 73.5 us -> 0.03 us  [local(): lax.all_gather(up_weight, 'ctx', axis=0, tiled=True)]
    all_gather x1, waiting for transfers between devices: 63.8 us -> 0.02 us  [local(): lax.all_gather(down_weight, 'ctx', axis=0, tiled=True)]
    all_gather x1, waiting for transfers between devices: 61.6 us -> 0.01 us  [local(): lax.all_gather(gate_weight, 'ctx', axis=0, tiled=True)]
    unnamed x7 -> x16, local copies, waits for them, and re-layouts: 1.51 us -> 20.5 us
    add x1 -> x0, other arithmetic: 13.5 us -> none  [local(): hidden_state = all_residual.astype(jnp.float32) + attn_total]
  transfers between devices with their start and end apart: 8 -> 10, of which waited for: 7 -> 6; matrix products, arithmetic and copies ran while one was open for 5% -> 11% of each run, Pallas kernels for 0% -> 0%
where the time goes in v1:
time: 480 us
  waiting for transfers between devices  294 us (61%)
  matrix products  116 us (24%)
  local copies, waits for them, and re-layouts  24.6 us (5%)
  other arithmetic  20.6 us (4%)
  between operations  15.2 us (3%)
  starting transfers between devices  9.76 us (2%)
    ppermute x3, waiting for transfers between devices, local(): lax.ppermute(ring[-1], 'tp', [(dev, (dev + 1) % 4) for dev in range(4)])  203 us
    reduce_scatter x1, waiting for transfers between devices, local(): lax.psum_scatter(lax.dot_general(hidden_units, down_full, (((1,), (1,)),...  80.3 us
    sub x1, matrix products, attend(): exponent = jnp.exp(scores - highest)  24.3 us
    dot_general x1, matrix products, local(): jnp.dot(head_out, out_weight, preferred_element_type=jnp.float32)  23.4 us
    dot_general x1, matrix products, local(): lax.dot_general(hidden_units, down_full, (((1,), (1,)), ((), ())), prefer...  22.5 us
    unnamed x16, local copies, waits for them, and re-layouts  20.5 us
    dot_general x1, matrix products, attend(): jnp.einsum('shl,kl->hsk', query_latent, keys_lat, preferred_element_type=...  18.1 us
    dot_general x1, matrix products, attend(): jnp.einsum('shl,hlv->shv', blended, value_up, preferred_element_type=jnp....  17.5 us
  transfers between devices with their start and end apart: 10, of which 6 were waited for; matrix products, arithmetic and copies ran while one was open for 11% of the time, Pallas kernels for 0%

profile of v1, /device:TPU:0, one launch (start us, length us, event | category | flops | bytes accessed | tf_op | source)
XLA Modules:
  0.0 480.0 jit_solution(12273457680901332404)
XLA Ops:
  7.4 0.5 collective-permute-start.3
  7.8 2.7 collective-permute-start.4
  10.5 0.8 fusion.35
  11.3 0.6 fusion.34
  11.9 1.3 fusion.22
  13.2 1.2 multiply_add_fusion
  14.4 1.2 broadcast_compare_fusion
  15.6 0.9 reshape.69
  16.5 1.5 copy.19
  18.0 0.1 copy.17
  18.1 1.5 collective-permute-done.4
  19.6 0.1 reshape.70
  19.7 0.1 copy.18
  19.9 18.1 %fusion.3 = f32[1024,512,16]{1,0,2:T(8,128)} fusion(bf16[512,16,512]{2,1,0:T(8,128)(2,1)} %param.12, bf16[512,512]{1,0:T(8,128)(2,1)} %collective-permute-done.3, bf16[512,512]{1,0:T(8,128)(2,1)} %param.14), kind=kOutput, calls=%fused_computation.11 | convolution fusion | flops 8592031744 | bytes 42991616 | tf_op jit(solution)/shard_map/while/body/eval_jaxpr/shl,kl->hsk/dot_general | solution.py:59
  37.9 24.3 %fusion.37 = (f32[16,512]{1,0:T(8,128)S(1)}, f32[16,512,1024]{1,2,0:T(8,128)}) fusion(f32[1024,512,16]{1,0,2:T(8,128)} %fusion.3, pred[512,1024]{0,1:T(8,128)(4,1)} %broadcast_compare_fusion, bf16[512,16,64]{0,2,1:T(8,128)(2,1)S(1)} %bitcast.36, bf16[512,64]{0,1:T(8,128)(2,1)S(1)} %copy.18, bf16[512,64]{0,1:T(8,128)(2,1)S(1)} %copy.17), kind=kOutput, calls=%fused_computation.59 | convolution fusion | flops 1115948032 | bytes 68845568 | tf_op jit(solution)/shard_map/while/body/eval_jaxpr/sub | solution.py:69
  62.2 17.5 %fusion.9 = bf16[16,512,128]{1,2,0:T(8,128)(2,1)} fusion(bf16[16,512,128]{2,1,0:T(8,128)(2,1)S(1)} %copy-done, f32[16,512,1024]{1,2,0:T(8,128)} %get-tuple-element.41, f32[16,512]{1,0:T(8,128)S(1)} %get-tuple-element.40, bf16[512,512]{1,0:T(8,128)(2,1)} %collective-permute-done.3, bf16[512,512]{1,0:T(8,128)(2,1)} %param.14), kind=kOutput, calls=%fused_computation.17 | convolution fusion | flops 9687793664 | bytes 38830080 | tf_op jit(solution)/shard_map/while/body/eval_jaxpr/shl,hlv->shv/dot_general | solution.py:74
  79.7 23.4 %convolution_convert_fusion.1 = bf16[512,7168]{1,0:T(8,128)(2,1)} fusion(bf16[512,2048]{0,1:T(8,128)(2,1)} %bitcast.37, bf16[2048,7168]{1,0:T(8,128)(2,1)} %param.18), kind=kOutput, calls=%fused_computation.10 | convolution fusion | flops 15036055552 | bytes 38797312 | tf_op jit(solution)/shard_map/dot_general | solution.py:84
  103.2 0.0 all-reduce.2.cloned.1.call-update
  103.2 0.0 all-gather.4.cloned.1.call-start
  103.2 0.5 all-gather.4.cloned.1.call-update
  103.8 0.0 all-gather.6.cloned.1.call-start
  103.8 0.5 all-gather.6.cloned.1.call-update
  104.4 0.0 all-gather.8.cloned.1.call-start
  104.4 2.1 collective-permute-start
  106.5 0.0 all-gather.8.cloned.1.call-update
  106.5 0.0 reduce-scatter.2.cloned.1.call-start
  106.6 77.9 %collective-permute-done = bf16[128,7168]{1,0:T(8,128)(2,1)} collective-permute-done((bf16[128,7168]{1,0:T(8,128)(2,1)S(1)}, bf16[128,7168]{1,0:T(8,128)(2,1)}, u32[]{:S(2)}, u32[]{:S(2)}) %collective-permute-start) | collective-permute-done | bytes 1835040 | tf_op jit(solution)/shard_map/ppermute | solution.py:88
  184.4 2.6 collective-permute-start.1
  187.0 57.5 %collective-permute-done.1 = bf16[128,7168]{1,0:T(8,128)(2,1)} collective-permute-done((bf16[128,7168]{1,0:T(8,128)(2,1)}, bf16[128,7168]{1,0:T(8,128)(2,1)}, u32[]{:S(2)}, u32[]{:S(2)}) %collective-permute-start.1) | collective-permute-done | bytes 1835040 | tf_op jit(solution)/shard_map/ppermute | solution.py:88
  244.6 1.8 collective-permute-start.2
  246.4 67.4 %collective-permute-done.2 = bf16[128,7168]{1,0:T(8,128)(2,1)} collective-permute-done((bf16[128,7168]{1,0:T(8,128)(2,1)}, bf16[128,7168]{1,0:T(8,128)(2,1)}, u32[]{:S(2)}, u32[]{:S(2)}) %collective-permute-start.2) | collective-permute-done | bytes 1835040 | tf_op jit(solution)/shard_map/ppermute | solution.py:88
  313.8 3.0 constant_dynamic-update-slice_fusion.7
  316.8 2.9 constant_dynamic-update-slice_fusion.6
  319.6 3.0 constant_dynamic-update-slice_fusion.5
  322.6 1.4 constant_dynamic-update-slice_fusion.4
  324.0 3.0 constant_dynamic-update-slice_fusion.3
  327.0 2.9 constant_dynamic-update-slice_fusion.2
  330.0 2.9 constant_dynamic-update-slice_fusion.1
  332.8 1.4 constant_dynamic-update-slice_fusion
  334.2 8.6 %all-reduce.2.cloned.1.call-done = bf16[512,7168]{1,0:T(8,128)(2,1)} async-done(((bf16[512,7168]{1,0:T(8,128)(2,1)}), bf16[512,7168]{1,0:T(8,128)(2,1)}) %all-reduce.2.cloned.1.call-update) | async-done | bytes 7340048 | tf_op jit(solution)/shard_map/psum | solution.py:85
  342.8 12.8 %multiply_reduce_fusion = (f32[512]{0:T(512)S(1)}, f32[512,7168]{1,0:T(8,128)}) fusion(bf16[512,7168]{1,0:T(8,128)(2,1)} %all-reduce.2.cloned.1.call-done, bf16[1024,7168]{1,0:T(8,128)(2,1)} %constant_dynamic-update-slice_fusion, s32[]{:T(128)S(6)} %select_n.57), kind=kLoop, calls=%fused_computation.6 | loop fusion | flops 18349568 | bytes 29362180 | tf_op jit(solution)/shard_map/reduce_sum | solution.py:13
  355.6 9.7 %fusion.33 = f32[512,512]{1,0:T(8,128)S(1)} fusion(bf16[7168,512]{1,0:T(8,128)(2,1)} %all-gather.4.cloned.1.call-done, f32[512,7168]{1,0:T(8,128)} %get-tuple-element.22, f32[7168]{0:T(1024)S(1)} %copy-done.3, f32[512]{0:T(512)S(1)} %add_rsqrt_fusion), kind=kOutput, calls=%fused_computation.55 | convolution fusion | flops 3769106432 | bytes 23099392 | tf_op jit(solution)/shard_map/dot_general | solution.py:100
  365.3 0.0 all-gather.6.cloned.1.call-done
  365.3 0.0 all-gather.8.cloned.1.call-done
  365.4 22.5 %convolution_convert_fusion = bf16[512,7168]{1,0:T(8,128)(2,1)} fusion(bf16[7168,512]{1,0:T(8,128)(2,1)} %all-gather.8.cloned.1.call-done, bf16[7168,512]{1,0:T(8,128)(2,1)} %all-gather.6.cloned.1.call-done, f32[512,512]{1,0:T(8,128)S(1)} %fusion.33, f32[512,7168]{1,0:T(8,128)} %get-tuple-element.22, f32[7168]{0:T(1024)S(1)} %copy-done.3, ...), kind=kOutput, calls=%fused_computation.9 | convolution fusion | flops 7532445696 | bytes 37779456 | tf_op jit(solution)/shard_map/dot_general | solution.py:104
  387.9 0.0 reduce-scatter.2.cloned.1.call-update
  387.9 80.3 %reduce-scatter.2.cloned.1.call-done = bf16[128,7168]{1,0:T(8,128)(2,1)} async-done(((bf16[512,7168]{1,0:T(8,128)(2,1)}), bf16[128,7168]{1,0:T(8,128)(2,1)}) %reduce-scatter.2.cloned.1.call-update) | async-done | bytes 1835024 | tf_op jit(solution)/shard_map/reduce_scatter | solution.py:103
  468.3 4.2 add_convert_fusion
  (13 shorter events, 0.0 us)
Async XLA Ops:
  7.4 54.8 %copy-start = (bf16[16,512,128]{2,1,0:T(8,128)(2,1)S(1)}, bf16[16,512,128]{2,1,0:T(8,128)(2,1)}, u32[]{:S(2)}) copy-start(bf16[16,512,128]{2,1,0:T(8,128)(2,1)} %param.17) | copy-start | bytes 6291460
  7.4 335.5 %all-reduce.2.cloned.1.call-start = ((), (), s32[]{:S(2)}) async-start(), calls=%async_computation.1 | async-start | bytes 14680064 | tf_op jit(solution)/shard_map/psum | solution.py:85
  7.4 12.5 %collective-permute-start.3 = (bf16[512,512]{1,0:T(8,128)(2,1)}, bf16[512,512]{1,0:T(8,128)(2,1)}, u32[]{:S(2)}, u32[]{:S(2)}) collective-permute-start(bf16[512,512]{1,0:T(8,128)(2,1)} %param.14), channel_id=1, source_target_pairs={{0,4},{4,8},{8,12},{12,16},{16,20},{20,24},{24,28},{28,0},{1,5},{5... | collective-permute-start | bytes 1572872 | tf_op jit(solution)/shard_map/ppermute | solution.py:9
  7.8 11.8 %collective-permute-start.4 = (bf16[256,128]{1,0:T(8,128)(2,1)}, bf16[256,128]{1,0:T(8,128)(2,1)S(1)}, u32[]{:S(2)}, u32[]{:S(2)}) collective-permute-start(bf16[256,128]{1,0:T(8,128)(2,1)} %param.15), channel_id=1, source_target_pairs={{0,4},{4,8},{8,12},{12,16},{16,20},{20,24},{24,28},{28,0},{1,5},{5... | collective-permute-start | bytes 196616 | tf_op jit(solution)/shard_map/ppermute | solution.py:9
  79.7 24.7 %copy-start.2 = (bf16[128,7168]{1,0:T(8,128)(2,1)S(1)}, bf16[128,7168]{1,0:T(8,128)(2,1)}, u32[]{:S(2)}) copy-start(bf16[128,7168]{1,0:T(8,128)(2,1)} %param.19) | copy-start | bytes 5505028
  103.2 252.4 %all-gather.4.cloned.1.call-start = ((), (), s32[]{:S(2)}) async-start(), calls=%async_computation.2 | async-start | bytes 8257536 | tf_op jit(solution)/shard_map/all_gather | solution.py:96
  103.8 261.6 %all-gather.6.cloned.1.call-start = ((), (), s32[]{:S(2)}) async-start(), calls=%async_computation.3 | async-start | bytes 8257536 | tf_op jit(solution)/shard_map/all_gather | solution.py:97
  104.4 261.0 %all-gather.8.cloned.1.call-start = ((), (), s32[]{:S(2)}) async-start(), calls=%async_computation.4 | async-start | bytes 8257536 | tf_op jit(solution)/shard_map/all_gather | solution.py:98
  104.4 80.0 %collective-permute-start = (bf16[128,7168]{1,0:T(8,128)(2,1)S(1)}, bf16[128,7168]{1,0:T(8,128)(2,1)}, u32[]{:S(2)}, u32[]{:S(2)}) collective-permute-start(bf16[128,7168]{1,0:T(8,128)(2,1)S(1)} %copy-done.2), channel_id=1, source_target_pairs={{0,1},{1,2},{2,3},{3,0},{4,5},{5,6},{6,7},{7,4},{8,9},{9,10},{10,1... | collective-permute-start | bytes 5505032 | tf_op jit(solution)/shard_map/ppermute | solution.py:88
  106.5 361.8 %reduce-scatter.2.cloned.1.call-start = ((), (), s32[]{:S(2)}) async-start(), calls=%async_computation.5 | async-start | bytes 9175040 | tf_op jit(solution)/shard_map/reduce_scatter | solution.py:103
  184.4 60.1 %collective-permute-start.1 = (bf16[128,7168]{1,0:T(8,128)(2,1)}, bf16[128,7168]{1,0:T(8,128)(2,1)}, u32[]{:S(2)}, u32[]{:S(2)}) collective-permute-start(bf16[128,7168]{1,0:T(8,128)(2,1)} %collective-permute-done), channel_id=1, source_target_pairs={{0,1},{1,2},{2,3},{3,0},{4,5},{5,6},{6,7},{7,4},{8,9},{9,10},{10,1... | collective-permute-start | bytes 5505032 | tf_op jit(solution)/shard_map/ppermute | solution.py:88
  244.6 69.2 %collective-permute-start.2 = (bf16[128,7168]{1,0:T(8,128)(2,1)}, bf16[128,7168]{1,0:T(8,128)(2,1)}, u32[]{:S(2)}, u32[]{:S(2)}) collective-permute-start(bf16[128,7168]{1,0:T(8,128)(2,1)} %collective-permute-done.1), channel_id=1, source_target_pairs={{0,1},{1,2},{2,3},{3,0},{4,5},{5,6},{6,7},{7,4},{8,9},{9,10},{10,1... | collective-permute-start | bytes 5505032 | tf_op jit(solution)/shard_map/ppermute | solution.py:88
  334.2 21.4 %copy-start.3 = (f32[7168]{0:T(1024)S(1)}, f32[7168]{0:T(1024)}, u32[]{:S(2)}) copy-start(f32[7168]{0:T(1024)} %param.20) | copy-start | bytes 86020
  365.4 107.1 %copy-start.1 = (bf16[16,512,128]{2,1,0:T(8,128)(2,1)S(1)}, bf16[16,512,128]{2,1,0:T(8,128)(2,1)}, u32[]{:S(2)}) copy-start(bf16[16,512,128]{2,1,0:T(8,128)(2,1)} %param.17) | copy-start | bytes 6291460
Sparse Core Ops, SparseCore 0:
  103.3 239.4 all-reduce.1
  388.0 80.1 reduce-scatter.1
Sparse Core Ops, SparseCore 1:
  105.3 73.2 all-gather.3
  180.0 71.8 all-gather.5
  253.4 71.8 all-gather.7
